TPU v7x, 32 devices: a whole 2x2x4 slice. The times are simulated.
32 devices in a mesh: ia: 4 (over y, x), ja: 8 (over z, core).
Axes of the slice: x: 2, y: 2, z: 4, core: 2. Of those that a mesh axis runs over, the one named last changes fastest.
Arguments:
- phase_space: float32 [12, 8192], P(None, 'ja'), may hold values from -6 to 6
- star_mass: float32 [8192], P('ja'), may hold values from 6.1035156e-05 to 0.00024414062
- star_level: int32 [8192], P('ja'), may hold values from 0 to 3
- active_ids: int32 [2, 64, 128], P(None, 'ia'), may hold values from 0 to 8191, as said below
- active_counts: int32 [2, 64], P(None, 'ia'), may hold values from 1 to 128, as said below
Outputs:
- final_state: float32 [12, 8192], P(None, 'ja')
- active_force: float32 [2, 6, 8192], P(None, None, ('ia', 'ja'))
Inputs may be any that keep to these rules, and one draw needn't show every extreme that they name: `active_ids`: within one block step the 64 x 128 entries are distinct star numbers; entries of unused slots are ignored. `active_counts`: in every block step one block is full and one holds a single star.
All inputs are finite; a program needn't handle non-finite values.
Results may differ from a plain program's by a relative error of at most 0.00018.
Values sent between devices are 32-bit elements; how exact they have to be, the bound alone decides.
A program may use at most 64 MiB of HBM per device.

v0:
```python
import jax
import jax.numpy as jnp
from jax import lax
from jax.sharding import PartitionSpec as P

STEPS = 2
EPS2 = 0.01
STEP_TIME = 0.05


def predict(state, tau):
    tau_sq = tau * tau
    tau_cube = tau_sq * tau
    new_pos = (
        state[0:3] + state[3:6] * tau + state[6:9] * (tau_sq * 0.5) + state[9:12] * (tau_cube / 6.0)
    )
    new_vel = state[3:6] + state[6:9] * tau + state[9:12] * (tau_sq * 0.5)
    return (new_pos, new_vel)


def field_force(target_pos, target_vel, source_pos, source_vel, source_mass):
    offset = source_pos[:, None, :] - target_pos[:, :, None]
    rel_vel = source_vel[:, None, :] - target_vel[:, :, None]
    dist_sq = jnp.sum(offset * offset, axis=0) + EPS2
    inverse = lax.rsqrt(dist_sq)
    weight = source_mass[None, :] * inverse * inverse * inverse
    radial = 3.0 * jnp.sum(offset * rel_vel, axis=0) / dist_sq
    accel = jnp.sum(weight[None] * offset, axis=2)
    jolt = jnp.sum(weight[None] * (rel_vel - radial[None] * offset), axis=2)
    return jnp.concatenate([accel, jolt], axis=0)


def blocked_force(target_pos, target_vel, source_pos, source_vel, source_mass, block_rows):
    total_rows = target_pos.shape[1]
    block_count = total_rows // block_rows
    tiles = (
        target_pos.reshape(3, block_count, block_rows).transpose(1, 0, 2),
        target_vel.reshape(3, block_count, block_rows).transpose(1, 0, 2),
    )

    def one_tile(pair_tile):
        return field_force(pair_tile[0], pair_tile[1], source_pos, source_vel, source_mass)

    result = lax.map(one_tile, tiles)
    return result.transpose(1, 0, 2).reshape(6, total_rows)


def correct(active_rows, accel, jolt, span):
    half_step = span * 0.5
    twelfth = span * span / 12.0
    old_pos = active_rows[0:3]
    old_vel = active_rows[3:6]
    old_acc = active_rows[6:9]
    old_jerk = active_rows[9:12]
    new_vel = old_vel + (old_acc + accel) * half_step + (old_jerk - jolt) * twelfth
    new_pos = old_pos + (old_vel + new_vel) * half_step + (old_acc - accel) * twelfth
    return jnp.concatenate([new_pos, new_vel, accel, jolt], axis=0)


def local(phase_space, star_mass, star_level, active_ids, active_counts):
    shard_width = phase_space.shape[1]
    shard_start = lax.axis_index("ja") * shard_width
    block_rows = 512
    state = phase_space
    last = -STEP_TIME * star_level.astype(jnp.float32)
    force_steps = []
    for step_index in range(STEPS):
        clock = STEP_TIME * (step_index + 1)
        indices = active_ids[step_index].reshape(-1)
        slot_pos = lax.broadcasted_iota(jnp.int32, (active_ids.shape[1], active_ids.shape[2]), 1)
        usable = (slot_pos < active_counts[step_index][:, None]).reshape(-1)
        local_ids = indices - shard_start
        inside = (local_ids >= 0) & (local_ids < shard_width)
        clipped = jnp.clip(local_ids, 0, shard_width - 1)
        fpos, fvel = predict(state, clock - last)
        stacked = jnp.concatenate([state, last[None, :]], axis=0)
        picked = jnp.where(inside[None, :], jnp.take(stacked, clipped, axis=1), 0.0)
        target_state = lax.psum(picked, "ja")
        tpos, tvel = predict(target_state[0:12], clock - target_state[12])
        partial_value = blocked_force(tpos, tvel, fpos, fvel, star_mass, block_rows)
        write_ids = jnp.where(usable, indices, -1)
        forces = lax.psum(partial_value, "ja")
        share_len = forces.shape[1] // lax.axis_size("ja")
        share_start = lax.axis_index("ja") * share_len
        force_share = lax.dynamic_slice_in_dim(forces, share_start, share_len, 1)
        usable_share = lax.dynamic_slice_in_dim(usable, share_start, share_len, 0)
        force_steps.append(jnp.where(usable_share[None, :], force_share, 0.0))
        outgoing = correct(target_state[0:12], forces[0:3], forces[3:6], clock - target_state[12])
        returned, return_ids = (
            lax.all_gather(outgoing, "ia", axis=1, tiled=True),
            lax.all_gather(write_ids, "ia", axis=0, tiled=True),
        )
        placed_raw = return_ids - shard_start
        valid = (return_ids >= 0) & (placed_raw >= 0) & (placed_raw < shard_width)
        placed = jnp.where(valid, placed_raw, shard_width)
        state = state.at[:, placed].set(returned, mode="drop")
        last = last.at[placed].set(clock, mode="drop")
    return (state, jnp.stack(force_steps))


def solution(mesh):
    placed = (P(None, "ja"), P("ja"), P("ja"), P(None, "ia", None), P(None, "ia"))
    return jax.shard_map(
        local,
        mesh=mesh,
        in_specs=placed,
        out_specs=(P(None, "ja"), P(None, None, ("ia", "ja"))),
        check_vma=False,
    )
```

profile of v0, /device:TPU:0, one launch (start us, length us, event | category | flops | bytes accessed | tf_op | source)
XLA Modules:
  0.0 312.5 jit_solution(17012939076392843902)
XLA Ops:
  11.3 5.5 %gather_fusion = f32[2048,13]{1,0:T(8,128)S(1)} fusion(f32[13,1024]{0,1:T(8,128)S(1)} %copy.110, s32[2048]{0:T(1024)S(1)} %get-tuple-element.164), kind=kCustom, calls=%fused_computation.clone | custom fusion | bytes 221184 | tf_op jit(solution)/shard_map/jit(_take)/gather | solution.py:77
  17.9 9.6 %all_gather.14 = s32[8192]{0:T(1024)S(1)} all-gather(s32[2048]{0:T(1024)S(1)} %get-tuple-element.165), channel_id=1, replica_groups=mesh['ia'=4,'ja'=8] {'ia'}, dimensions={0}, use_global_device_ids=true | all-gather | bytes 40960 | tf_op jit(solution)/shard_map/all_gather | solution.py:91
  27.5 8.1 %all_gather.12 = s32[8192]{0:T(1024)S(1)} all-gather(s32[2048]{0:T(1024)S(1)} %get-tuple-element.166), channel_id=1, replica_groups=mesh['ia'=4,'ja'=8] {'ia'}, dimensions={0}, use_global_device_ids=true | all-gather | bytes 40960 | tf_op jit(solution)/shard_map/all_gather | solution.py:91
  35.7 30.4 %scatter_fusion.1 = f32[1024]{0:T(1024)S(1)} fusion(f32[1024]{0:T(1024)S(1)} %get-tuple-element.170, s32[8192]{0:T(1024)S(1)} %compare_select_fusion.1, f32[8192]{0:T(1024)S(1)} %broadcast.175), kind=kCustom, calls=%fused_computation.3 | custom fusion | bytes 131072 | tf_op jit(solution)/shard_map/scatter | solution.py:97
  66.9 7.9 %all-reduce.3.cloned.1.call-done = f32[13,2048]{1,0:T(8,128)} async-done(((f32[13,2048]{1,0:T(8,128)}), f32[13,2048]{1,0:T(8,128)}) %all-reduce.3.cloned.1.call-update) | async-done | bytes 106512 | tf_op jit(solution)/shard_map/psum | solution.py:78
  76.8 20.9 %while.20 = (s32[]{:T(128)}, f32[4,6,512]{2,1,0:T(8,128)S(1)}, f32[1024]{0:T(1024)S(1)}, f32[3,1024]{1,0:T(4,128)S(1)}, f32[4,3,512]{2,1,0:T(4,128)S(1)}, /*inde...) while((s32[]{:T(128)}, f32[4,6,512]{2,1,0:T(8,128)S(1)}, f32[1024]{0:T(1024)S(1)}, ...), condition=%wide.region_6.8_spmd, body=%wide.region_1.7_spmd.sunk | while | flops 24117248 | bytes 16924772 | solution.py:44
  79.5 2.4 fusion.32
  84.8 2.4 fusion.32
  90.0 2.4 fusion.32
  95.2 2.4 fusion.32
  97.7 26.3 %psum.29 = f32[6,2048]{1,0:T(8,128)S(1)} all-reduce(f32[6,2048]{1,0:T(8,128)S(1)} %bitcast.106), channel_id=1, replica_groups=mesh['ia'=4,'ja'=8] {'ja'}, use_global_device_ids=true, to_apply=%region_7.9 | all-reduce | flops 12288 | bytes 98304 | tf_op jit(solution)/shard_map/psum | solution.py:82
  124.1 10.0 %all_gather.13 = f32[12,8192]{1,0:T(8,128)S(1)} all-gather(f32[12,2048]{1,0:T(8,128)S(1)} %pad_maximum_fusion.1), channel_id=1, replica_groups=mesh['ia'=4,'ja'=8] {'ia'}, dimensions={1}, use_global_device_ids=true | all-gather | bytes 491520 | tf_op jit(solution)/shard_map/all_gather | solution.py:90
  134.1 2.6 copy.115
  136.8 21.2 %scatter_fusion = f32[12,1024]{0,1:T(8,128)S(1)} fusion(f32[12,1024]{0,1:T(8,128)S(1)} %copy.114, s32[8192]{0:T(1024)S(1)} %compare_select_fusion.1, f32[8192,12]{1,0:T(8,128)} %copy.115), kind=kCustom, calls=%fused_computation.2 | custom fusion | bytes 1212416 | tf_op jit(solution)/shard_map/scatter | solution.py:96
  159.5 7.6 %gather_fusion.1 = f32[2048,13]{1,0:T(8,128)} fusion(f32[13,1024]{0,1:T(8,128)S(1)} %pad_maximum_fusion, s32[2048]{0:T(1024)S(1)} %get-tuple-element.163), kind=kCustom, calls=%fused_computation.1.clone | custom fusion | bytes 221184 | tf_op jit(solution)/shard_map/jit(_take)/gather | solution.py:77
  171.2 50.0 %all-reduce.5.cloned.1.call-done = f32[13,2048]{1,0:T(8,128)} async-done(((f32[13,2048]{1,0:T(8,128)}), f32[13,2048]{1,0:T(8,128)}) %all-reduce.5.cloned.1.call-update) | async-done | bytes 106512 | tf_op jit(solution)/shard_map/psum | solution.py:78
  223.1 20.9 %while.21 = (s32[]{:T(128)}, f32[4,6,512]{2,1,0:T(8,128)S(1)}, f32[1024]{0:T(1024)S(1)}, f32[3,1024]{1,0:T(4,128)S(1)}, f32[4,3,512]{2,1,0:T(4,128)S(1)}, /*inde...) while((s32[]{:T(128)}, f32[4,6,512]{2,1,0:T(8,128)S(1)}, f32[1024]{0:T(1024)S(1)}, ...), condition=%wide.region_16.18_spmd, body=%wide.region_11.17_spmd.sunk | while | flops 24117248 | bytes 16924772 | solution.py:44
  225.9 2.4 fusion.35
  231.2 2.4 fusion.35
  236.4 2.4 fusion.35
  244.1 26.3 %psum.31 = f32[6,2048]{1,0:T(8,128)S(1)} all-reduce(f32[6,2048]{1,0:T(8,128)S(1)} %bitcast.105), channel_id=1, replica_groups=mesh['ia'=4,'ja'=8] {'ja'}, use_global_device_ids=true, to_apply=%region_17.19 | all-reduce | flops 12288 | bytes 98304 | tf_op jit(solution)/shard_map/psum | solution.py:82
  270.6 10.0 %all_gather.15 = f32[12,8192]{1,0:T(8,128)S(1)} all-gather(f32[12,2048]{1,0:T(8,128)S(1)} %pad_maximum_fusion.2), channel_id=1, replica_groups=mesh['ia'=4,'ja'=8] {'ia'}, dimensions={1}, use_global_device_ids=true | all-gather | bytes 491520 | tf_op jit(solution)/shard_map/all_gather | solution.py:90
  280.6 2.6 copy.124
  283.2 21.1 %scatter_fusion.2 = f32[12,1024]{0,1:T(8,128)S(1)} fusion(f32[12,1024]{0,1:T(8,128)S(1)} %scatter_fusion, s32[8192]{0:T(1024)S(1)} %compare_select_fusion, f32[8192,12]{1,0:T(8,128)} %copy.124), kind=kCustom, calls=%fused_computation.4 | custom fusion | bytes 1212416 | tf_op jit(solution)/shard_map/scatter | solution.py:96
  (89 shorter events, 41.4 us)
Async XLA Ops:
  7.2 67.6 %all-reduce.3.cloned.1.call-start = ((), (), s32[]{:S(2)}) async-start(), calls=%async_computation | async-start | bytes 262144 | tf_op jit(solution)/shard_map/psum | solution.py:78
  17.8 203.4 %all-reduce.5.cloned.1.call-start = ((), (), s32[]{:S(2)}) async-start(), calls=%async_computation.1 | async-start | bytes 262144 | tf_op jit(solution)/shard_map/psum | solution.py:78
  35.7 30.5 %copy-start = (f32[12,1024]{1,0:T(8,128)S(1)}, f32[12,1024]{1,0:T(8,128)}, u32[]{:S(2)}) copy-start(f32[12,1024]{1,0:T(8,128)} %param.11) | copy-start | bytes 147460
  35.7 41.0 %copy-start.3 = (f32[1024]{0:T(1024)S(1)}, f32[1024]{0:T(1024)}, u32[]{:S(2)}) copy-start(f32[1024]{0:T(1024)} %param.12) | copy-start | bytes 12292
  76.7 47.3 %copy-start.1 = (f32[13,2048]{1,0:T(8,128)S(1)}, f32[13,2048]{1,0:T(8,128)}, u32[]{:S(2)}) copy-start(f32[13,2048]{1,0:T(8,128)} %all-reduce.3.cloned.1.call-done) | copy-start | bytes 319492
  223.1 47.3 %copy-start.2 = (f32[13,2048]{1,0:T(8,128)S(1)}, f32[13,2048]{1,0:T(8,128)}, u32[]{:S(2)}) copy-start(f32[13,2048]{1,0:T(8,128)} %all-reduce.5.cloned.1.call-done) | copy-start | bytes 319492
Sparse Core Ops, SparseCore 0:
  17.9 56.8 all-reduce.2
  169.4 51.7 all-reduce.4
where the time goes:
time: 313 us
  local copies, waits for them, and re-layouts  98.5 us (31%)
  blocking collectives  90.4 us (29%)
  waiting for transfers between devices  57.9 us (18%)
  other arithmetic  50.9 us (16%)
  between operations  14.3 us (5%)
    psum x2, waiting for transfers between devices, local(): target_state = lax.psum(picked, 'ja')  57.9 us
    psum x2, blocking collectives, local(): forces = lax.psum(partial_value, 'ja')  52.7 us
    scatter x2, local copies, waits for them, and re-layouts, local(): state = state.at[:, placed].set(returned, mode='drop')  42.3 us
    scatter x1, local copies, waits for them, and re-layouts, local(): last = last.at[placed].set(clock, mode='drop')  30.4 us
    all_gather x2, blocking collectives, local(): lax.all_gather(outgoing, 'ia', axis=1, tiled=True)  20 us
    reduce_sum x8, other arithmetic, field_force(): accel = jnp.sum(weight[None] * offset, axis=2)  19.5 us
    all_gather x2, blocking collectives, local(): lax.all_gather(write_ids, 'ia', axis=0, tiled=True)  17.7 us
    gather x4, local copies, waits for them, and re-layouts, local(): picked = jnp.where(inside[None, :], jnp.take(stacked, clipped, axis=1), 0.0)  14.9 us
  transfers between devices with their start and end apart: 2, of which 2 were waited for; matrix products, arithmetic and copies ran while one was open for 11% of the time, Pallas kernels for 0%

commit v1 on v0

--- a/solution.py
+++ b/solution.py
@@ -6,6 +6,24 @@
 STEPS = 2
 EPS2 = 0.01
 STEP_TIME = 0.05
+
+
+def collect(shard, axis, dim):
+    ways, here, turn = (lax.axis_size(axis), lax.axis_index(axis), shard.shape[dim])
+    dims = [n * ways if d == dim else n for d, n in enumerate(shard.shape)]
+    full = lax.dynamic_update_slice_in_dim(
+        jnp.zeros(dims, shard.dtype), shard, here * turn, axis=dim
+    )
+    going_up = going_down = shard
+    for far in range(1, ways // 2 + 1):
+        going_up = lax.ppermute(going_up, axis, [(d, (d + 1) % ways) for d in range(ways)])
+        full = lax.dynamic_update_slice_in_dim(full, going_up, (here - far) % ways * turn, axis=dim)
+        if 2 * far < ways:
+            going_down = lax.ppermute(going_down, axis, [(d, (d - 1) % ways) for d in range(ways)])
+            full = lax.dynamic_update_slice_in_dim(
+                full, going_down, (here + far) % ways * turn, axis=dim
+            )
+    return full
 
 
 def predict(state, tau):
@@ -88,7 +106,7 @@
         outgoing = correct(target_state[0:12], forces[0:3], forces[3:6], clock - target_state[12])
         returned, return_ids = (
             lax.all_gather(outgoing, "ia", axis=1, tiled=True),
-            lax.all_gather(write_ids, "ia", axis=0, tiled=True),
+            collect(write_ids, "ia", 0),
         )
         placed_raw = return_ids - shard_start
         valid = (return_ids >= 0) & (placed_raw >= 0) & (placed_raw < shard_width)

time: 313 us -> 319 us (1.019)
  blocking collectives: 90.4 us -> 72.7 us
  waiting for transfers between devices: 57.9 us -> 68 us
  starting transfers between devices: 0.08 us -> 9.49 us
    all_gather x2 -> x0, blocking collectives: 17.7 us -> none  [local(): lax.all_gather(write_ids, 'ia', axis=0, tiled=True)]
    ppermute x0 -> x6, starting transfers between devices: none -> 9.41 us  [the longest x4 6.43 us: collect(): lax.ppermute(going_up, axis, [(d, (d + 1) % ways) for d in range(ways)])]
    psum x2, waiting for transfers between devices: 57.9 us -> 66.3 us  [local(): target_state = lax.psum(picked, 'ja')]
  transfers between devices with their start and end apart: 2 -> 8, of which waited for: 2 -> 3; matrix products, arithmetic and copies ran while one was open for 11% -> 14% of each run, Pallas kernels for 0% -> 0%
where the time goes in v1:
time: 319 us; the launch traced here: 318 us
  local copies, waits for them, and re-layouts  101 us (32%)
  blocking collectives  72.7 us (23%)
  waiting for transfers between devices  68 us (21%)
  other arithmetic  52.5 us (16%)
  between operations  14.4 us (5%)
  starting transfers between devices  9.49 us (3%)
    psum x2, waiting for transfers between devices, local(): target_state = lax.psum(picked, 'ja')  66.3 us
    psum x2, blocking collectives, local(): forces = lax.psum(partial_value, 'ja')  52.7 us
    scatter x2, local copies, waits for them, and re-layouts, local(): state = state.at[:, placed].set(returned, mode='drop')  42.3 us
    scatter x1, local copies, waits for them, and re-layouts, local(): last = last.at[placed].set(clock, mode='drop')  30.4 us
    all_gather x2, blocking collectives, local(): lax.all_gather(outgoing, 'ia', axis=1, tiled=True)  20 us
    reduce_sum x8, other arithmetic, field_force(): accel = jnp.sum(weight[None] * offset, axis=2)  19.5 us
    gather x4, local copies, waits for them, and re-layouts, local(): picked = jnp.where(inside[None, :], jnp.take(stacked, clipped, axis=1), 0.0)  14.9 us
    reduce_sum x8, other arithmetic, field_force(): dist_sq = jnp.sum(offset * offset, axis=0) + EPS2  14.3 us
  transfers between devices with their start and end apart: 8, of which 3 were waited for; matrix products, arithmetic and copies ran while one was open for 14% of the time, Pallas kernels for 0%

profile of v1, /device:TPU:0, one launch (start us, length us, event | category | flops | bytes accessed | tf_op | source)
XLA Modules:
  0.0 318.4 jit_solution(11413549491038646791)
XLA Ops:
  8.7 2.9 collective-permute-start
  18.0 5.5 %gather_fusion = f32[2048,13]{1,0:T(8,128)S(1)} fusion(f32[13,1024]{0,1:T(8,128)S(1)} %copy.110, s32[2048]{0:T(1024)S(1)} %get-tuple-element.168), kind=kCustom, calls=%fused_computation.clone | custom fusion | bytes 221184 | tf_op jit(solution)/shard_map/jit(_take)/gather | solution.py:95
  33.6 30.4 %scatter_fusion.1 = f32[1024]{0:T(1024)S(1)} fusion(f32[1024]{0:T(1024)S(1)} %get-tuple-element.174, s32[8192]{0:T(1024)S(1)} %compare_select_fusion.1, f32[8192]{0:T(1024)S(1)} %broadcast.178), kind=kCustom, calls=%fused_computation.3 | custom fusion | bytes 131072 | tf_op jit(solution)/shard_map/scatter | solution.py:115
  64.3 16.3 %all-reduce.3.cloned.1.call-done = f32[13,2048]{1,0:T(8,128)} async-done(((f32[13,2048]{1,0:T(8,128)}), f32[13,2048]{1,0:T(8,128)}) %all-reduce.3.cloned.1.call-update) | async-done | bytes 106512 | tf_op jit(solution)/shard_map/psum | solution.py:96
  82.6 20.9 %while.20 = (s32[]{:T(128)}, f32[4,6,512]{2,1,0:T(8,128)S(1)}, f32[1024]{0:T(1024)S(1)}, f32[3,1024]{1,0:T(4,128)S(1)}, f32[4,3,512]{2,1,0:T(4,128)S(1)}, /*inde...) while((s32[]{:T(128)}, f32[4,6,512]{2,1,0:T(8,128)S(1)}, f32[1024]{0:T(1024)S(1)}, ...), condition=%wide.region_6.8_spmd, body=%wide.region_1.7_spmd.sunk | while | flops 24117248 | bytes 16924772 | solution.py:62
  85.4 2.4 fusion.34
  90.6 2.4 fusion.34
  95.8 2.4 fusion.34
  101.1 2.4 fusion.34
  103.5 26.3 %psum.29 = f32[6,2048]{1,0:T(8,128)S(1)} all-reduce(f32[6,2048]{1,0:T(8,128)S(1)} %bitcast.110), channel_id=1, replica_groups=mesh['ia'=4,'ja'=8] {'ja'}, use_global_device_ids=true, to_apply=%region_7.9 | all-reduce | flops 12288 | bytes 98304 | tf_op jit(solution)/shard_map/psum | solution.py:100
  130.0 10.0 %all_gather.6 = f32[12,8192]{1,0:T(8,128)S(1)} all-gather(f32[12,2048]{1,0:T(8,128)S(1)} %pad_maximum_fusion.1), channel_id=1, replica_groups=mesh['ia'=4,'ja'=8] {'ia'}, dimensions={1}, use_global_device_ids=true | all-gather | bytes 491520 | tf_op jit(solution)/shard_map/all_gather | solution.py:108
  140.0 2.6 copy.115
  142.6 21.2 %scatter_fusion = f32[12,1024]{0,1:T(8,128)S(1)} fusion(f32[12,1024]{0,1:T(8,128)S(1)} %copy.114, s32[8192]{0:T(1024)S(1)} %compare_select_fusion.1, f32[8192,12]{1,0:T(8,128)} %copy.115), kind=kCustom, calls=%fused_computation.2 | custom fusion | bytes 1212416 | tf_op jit(solution)/shard_map/scatter | solution.py:114
  165.3 7.6 %gather_fusion.1 = f32[2048,13]{1,0:T(8,128)} fusion(f32[13,1024]{0,1:T(8,128)S(1)} %pad_maximum_fusion, s32[2048]{0:T(1024)S(1)} %get-tuple-element.167), kind=kCustom, calls=%fused_computation.1.clone | custom fusion | bytes 221184 | tf_op jit(solution)/shard_map/jit(_take)/gather | solution.py:95
  177.1 50.0 %all-reduce.5.cloned.1.call-done = f32[13,2048]{1,0:T(8,128)} async-done(((f32[13,2048]{1,0:T(8,128)}), f32[13,2048]{1,0:T(8,128)}) %all-reduce.5.cloned.1.call-update) | async-done | bytes 106512 | tf_op jit(solution)/shard_map/psum | solution.py:96
  229.0 20.9 %while.21 = (s32[]{:T(128)}, f32[4,6,512]{2,1,0:T(8,128)S(1)}, f32[1024]{0:T(1024)S(1)}, f32[3,1024]{1,0:T(4,128)S(1)}, f32[4,3,512]{2,1,0:T(4,128)S(1)}, /*inde...) while((s32[]{:T(128)}, f32[4,6,512]{2,1,0:T(8,128)S(1)}, f32[1024]{0:T(1024)S(1)}, ...), condition=%wide.region_16.18_spmd, body=%wide.region_11.17_spmd.sunk | while | flops 24117248 | bytes 16924772 | solution.py:62
  231.8 2.4 fusion.37
  237.0 2.4 fusion.37
  242.2 2.4 fusion.37
  247.5 2.4 fusion.37
  249.9 26.3 %psum.31 = f32[6,2048]{1,0:T(8,128)S(1)} all-reduce(f32[6,2048]{1,0:T(8,128)S(1)} %bitcast.109), channel_id=1, replica_groups=mesh['ia'=4,'ja'=8] {'ja'}, use_global_device_ids=true, to_apply=%region_17.19 | all-reduce | flops 12288 | bytes 98304 | tf_op jit(solution)/shard_map/psum | solution.py:100
  276.4 10.0 %all_gather.7 = f32[12,8192]{1,0:T(8,128)S(1)} all-gather(f32[12,2048]{1,0:T(8,128)S(1)} %pad_maximum_fusion.2), channel_id=1, replica_groups=mesh['ia'=4,'ja'=8] {'ia'}, dimensions={1}, use_global_device_ids=true | all-gather | bytes 491520 | tf_op jit(solution)/shard_map/all_gather | solution.py:108
  286.4 2.6 copy.124
  289.0 21.1 %scatter_fusion.2 = f32[12,1024]{0,1:T(8,128)S(1)} fusion(f32[12,1024]{0,1:T(8,128)S(1)} %scatter_fusion, s32[8192]{0:T(1024)S(1)} %compare_select_fusion, f32[8192,12]{1,0:T(8,128)} %copy.124), kind=kCustom, calls=%fused_computation.4 | custom fusion | bytes 1212416 | tf_op jit(solution)/shard_map/scatter | solution.py:114
  (106 shorter events, 51.2 us)
Async XLA Ops:
  7.2 73.5 %all-reduce.3.cloned.1.call-start = ((), (), s32[]{:S(2)}) async-start(), calls=%async_computation | async-start | bytes 262144 | tf_op jit(solution)/shard_map/psum | solution.py:96
  8.7 16.8 %collective-permute-start = (s32[2048]{0:T(1024)S(1)}, s32[2048]{0:T(1024)S(1)}, u32[]{:S(2)}, u32[]{:S(2)}) collective-permute-start(s32[2048]{0:T(1024)S(1)} %get-tuple-element.132), channel_id=1, source_target_pairs={{0,8},{8,16},{16,24},{24,0},{1,9},{9,17},{17,25},{25,1},{2,10},{10... | collective-permute-start | bytes 24584 | tf_op jit(solution)/shard_map/ppermute | solution.py:19
  11.7 19.1 %collective-permute-start.1 = (s32[2048]{0:T(1024)S(1)}, s32[2048]{0:T(1024)S(1)}, u32[]{:S(2)}, u32[]{:S(2)}) collective-permute-start(s32[2048]{0:T(1024)S(1)} %get-tuple-element.132), channel_id=1, source_target_pairs={{0,24},{8,0},{16,8},{24,16},{1,25},{9,1},{17,9},{25,17},{2,26},{10... | collective-permute-start | bytes 24584 | tf_op jit(solution)/shard_map/ppermute | solution.py:22
  13.4 17.7 %collective-permute-start.4 = (s32[2048]{0:T(1024)S(1)}, s32[2048]{0:T(1024)S(1)}, u32[]{:S(2)}, u32[]{:S(2)}) collective-permute-start(s32[2048]{0:T(1024)S(1)} %get-tuple-element.170), channel_id=1, source_target_pairs={{0,24},{8,0},{16,8},{24,16},{1,25},{9,1},{17,9},{25,17},{2,26},{10... | collective-permute-start | bytes 24584 | tf_op jit(solution)/shard_map/ppermute | solution.py:22
  15.5 13.4 %collective-permute-start.3 = (s32[2048]{0:T(1024)S(1)}, s32[2048]{0:T(1024)S(1)}, u32[]{:S(2)}, u32[]{:S(2)}) collective-permute-start(s32[2048]{0:T(1024)S(1)} %get-tuple-element.170), channel_id=1, source_target_pairs={{0,8},{8,16},{16,24},{24,0},{1,9},{9,17},{17,25},{25,1},{2,10},{10... | collective-permute-start | bytes 24584 | tf_op jit(solution)/shard_map/ppermute | solution.py:19
  24.5 202.6 %all-reduce.5.cloned.1.call-start = ((), (), s32[]{:S(2)}) async-start(), calls=%async_computation.1 | async-start | bytes 262144 | tf_op jit(solution)/shard_map/psum | solution.py:96
  25.5 5.9 %collective-permute-start.2 = (s32[2048]{0:T(1024)S(1)}, s32[2048]{0:T(1024)S(1)}, u32[]{:S(2)}, u32[]{:S(2)}) collective-permute-start(s32[2048]{0:T(1024)S(1)} %collective-permute-done), channel_id=1, source_target_pairs={{0,8},{8,16},{16,24},{24,0},{1,9},{9,17},{17,25},{25,1},{2,10},{10... | collective-permute-start | bytes 24584 | tf_op jit(solution)/shard_map/ppermute | solution.py:19
  28.9 4.6 %collective-permute-start.5 = (s32[2048]{0:T(1024)S(1)}, s32[2048]{0:T(1024)S(1)}, u32[]{:S(2)}, u32[]{:S(2)}) collective-permute-start(s32[2048]{0:T(1024)S(1)} %collective-permute-done.3), channel_id=1, source_target_pairs={{0,8},{8,16},{16,24},{24,0},{1,9},{9,17},{17,25},{25,1},{2,10},{10... | collective-permute-start | bytes 24584 | tf_op jit(solution)/shard_map/ppermute | solution.py:19
  33.6 49.0 %copy-start.2 = (f32[1024]{0:T(1024)S(1)}, f32[1024]{0:T(1024)}, u32[]{:S(2)}) copy-start(f32[1024]{0:T(1024)} %param.12) | copy-start | bytes 12292
  82.6 47.3 %copy-start = (f32[13,2048]{1,0:T(8,128)S(1)}, f32[13,2048]{1,0:T(8,128)}, u32[]{:S(2)}) copy-start(f32[13,2048]{1,0:T(8,128)} %all-reduce.3.cloned.1.call-done) | copy-start | bytes 319492
  229.0 47.3 %copy-start.1 = (f32[13,2048]{1,0:T(8,128)S(1)}, f32[13,2048]{1,0:T(8,128)}, u32[]{:S(2)}) copy-start(f32[13,2048]{1,0:T(8,128)} %all-reduce.5.cloned.1.call-done) | copy-start | bytes 319492
Sparse Core Ops, SparseCore 0:
  24.6 55.9 all-reduce.2
  175.3 51.7 all-reduce.4
